TPU v7x, 32 devices: a whole 2x2x4 slice. The times are simulated.
32 devices in a mesh: angle: 4 (over x, core), gz: 8 (over z, y).
Axes of the slice: x: 2, y: 2, z: 4, core: 2. Of those that a mesh axis runs over, the one named last changes fastest.
Arguments:
- projections: bfloat16 [48, 128, 4096], P('angle', 'gz'), may hold values from -6 to 6
- partner_view: int32 [48], P('angle'), may hold values from 0 to 47, as said below
- row_weight: bfloat16 [48, 128], P('angle', 'gz'), may hold values from 0.099609375 to 1
- row_slab: int32 [48, 128], P('angle', 'gz'), may hold values from 0 to 127, as said below
Outputs:
- slab_sinogram: bfloat16 [48, 128, 8192], P('angle', 'gz')
Inputs may be any that keep to these rules, and one draw needn't show every extreme that they name: `partner_view`: the partner of a view lies in the block of 12 views whose block index differs by half the number of blocks (2); the partner of the partner is the view itself. `row_slab`: owner of slab s is s // 16. Among the 12 x 16 rows of one device (one block of views and one block of detector rows), at most 48 go to the slabs of any one owner; in every draw, for each block of views, some owner receives exactly 48 rows from every block of detector rows.
All inputs are finite; a program needn't handle non-finite values.
Results may differ from a plain program's by a relative error of at most 0.001.
Values may be sent and summed in bfloat16 or wider, within the bound.
A program may use at most 128 MiB of HBM per device.

v0:
```python
import functools
import math

import jax
import jax.numpy as jnp
from jax import lax
from jax.experimental import pallas as pl
from jax.experimental.pallas import tpu as pltpu
from jax.sharding import PartitionSpec as P
import ml_dtypes
import numpy as np

OV = 128
KB = 256
SLAB_DEV = 16
CHUNKS = 2
BF = jnp.bfloat16
F32 = jnp.float32
MESH = pl.DeviceIdType.MESH


def taps(size):
    offset = np.arange(size)[None, :] + size - np.arange(3 * size)[:, None]
    squared = np.maximum(offset.astype(np.float64) ** 2, 1.0)
    values = np.where(
        offset == 0, 0.25, np.where(offset % 2 != 0, -1.0 / (math.pi * math.pi * squared), 0.0)
    )
    return np.where(np.abs(offset) <= size, values, 0.0).astype(np.float32)


def exchange_kernel(
    owners, blocks, chunk, raw_ref, pick_own_ref, pick_mirror_ref, flip_ref, got_ref,
    flipped, outgoing, send_sem, recv_sem, local_sem,
):
    me_a, me_g = lax.axis_index("angle"), lax.axis_index("gz")
    partner = lax.rem(me_a + blocks // 2, blocks)
    slots = outgoing.shape[3]
    channels = raw_ref.shape[1]
    barrier = pltpu.get_barrier_semaphore()
    for kind in range(2):
        target_a = me_a if kind == 0 else partner
        for step in range(1 - kind, owners):
            pl.semaphore_signal(
                barrier, inc=1, device_id=(target_a, lax.rem(me_g + step, owners)),
                device_id_type=MESH,
            )
    width = 2 * KB
    for at in range(channels // KB):
        block = jnp.dot(raw_ref[:, at * KB:(at + 1) * KB], flip_ref[...], preferred_element_type=F32)
        to = channels - (at + 1) * KB
        flipped[:, to:to + KB] = block.astype(BF)
    pl.semaphore_wait(barrier, 2 * owners - 1)
    copies = []
    for part in range(channels // chunk):
        for kind in range(2):
            pick = pick_own_ref if kind == 0 else pick_mirror_ref
            source = raw_ref if kind == 0 else flipped
            for at in range(chunk // width):
                begin = part * chunk + at * width
                rows = jnp.dot(pick[...], source[:, begin:begin + width], preferred_element_type=F32)
                rows = rows.astype(BF).reshape(owners, slots, width)
                outgoing[part, kind, :, :, at * width:(at + 1) * width] = rows
            target_a = me_a if kind == 0 else partner
            for step in range(owners - 1, -1, -1):
                to = lax.rem(me_g + step, owners)
                if kind == 0 and step == 0:
                    copy = pltpu.make_async_copy(
                        outgoing.at[part, kind, me_g], got_ref.at[part, kind, me_g],
                        local_sem.at[part],
                    )
                else:
                    copy = pltpu.make_async_remote_copy(
                        src_ref=outgoing.at[part, kind, to],
                        dst_ref=got_ref.at[part, kind, me_g],
                        send_sem=send_sem.at[part, kind, step],
                        recv_sem=recv_sem.at[part, kind, step],
                        device_id=(target_a, to),
                        device_id_type=MESH,
                    )
                copy.start()
                copies.append(copy)
    for copy in copies:
        copy.wait()


def exchange(raw, pick_own, pick_mirror, flip, owners, blocks, slots):
    rows, channels = raw.shape
    chunk = channels // CHUNKS
    vmem = pl.BlockSpec(memory_space=pltpu.VMEM)
    return pl.pallas_call(
        functools.partial(exchange_kernel, owners, blocks, chunk),
        out_shape=jax.ShapeDtypeStruct((CHUNKS, 2, owners, slots, chunk), BF),
        in_specs=[vmem] * 4,
        out_specs=pl.BlockSpec(memory_space=pl.ANY),
        scratch_shapes=[
            pltpu.VMEM((rows, channels), BF),
            pltpu.VMEM((CHUNKS, 2, owners, slots, chunk), BF),
            pltpu.SemaphoreType.DMA((CHUNKS, 2, owners)),
            pltpu.SemaphoreType.DMA((CHUNKS, 2, owners)),
            pltpu.SemaphoreType.DMA((CHUNKS,)),
        ],
        compiler_params=pltpu.CompilerParams(
            collective_id=0, has_side_effects=True, vmem_limit_bytes=48 * 2**20
        ),
        name="exchange",
    )(raw, pick_own, pick_mirror, flip)


def filter_kernel(got_ref, sum_ref, high_ref, low_ref, feather_ref, out_ref, high, low):
    parts, _, _, chunk = got_ref.shape
    channels = parts * chunk
    count = channels // KB
    pad = 2 * KB
    for ref in (high, low):
        ref[:, :pad] = jnp.zeros((ref.shape[0], pad), BF)
        ref[:, ref.shape[1] - pad:] = jnp.zeros((ref.shape[0], pad), BF)

    def summed(kind, at):
        part, begin = at * KB // chunk, at * KB % chunk
        return jnp.dot(
            sum_ref[...], got_ref[part, kind, :, begin:begin + KB], preferred_element_type=F32
        )

    for at in range(2 * count - 1):
        if at < count - 1:
            value = summed(1, at)
        elif at >= count:
            value = summed(0, at - count + 1)
        else:
            weight = feather_ref[...]
            value = weight * summed(0, 0) + (1.0 - weight) * summed(1, at)
        top = value.astype(BF)
        place = pl.ds(pad + at * KB, KB)
        high[:, place] = top
        low[:, place] = (value - top.astype(F32)).astype(BF)
    for at in range(-1, 2 * count):
        window = pl.ds(pad + (at - 1) * KB, 3 * KB)
        value = jnp.dot(high[:, window], high_ref[...], preferred_element_type=F32)
        value += jnp.dot(high[:, window], low_ref[...], preferred_element_type=F32)
        value += jnp.dot(low[:, window], high_ref[...], preferred_element_type=F32)
        value = value.astype(BF)
        begin = OV + at * KB
        if at < 0:
            out_ref[:, :OV] = value[:, OV:]
        elif at == 2 * count - 1:
            out_ref[:, begin:] = value[:, :OV]
        else:
            out_ref[:, begin:begin + KB] = value


def filtered_slabs(got, sums, feather):
    parts, kinds, owners, slots, chunk = got.shape
    channels = parts * chunk
    rows = sums.shape[0]
    tap = taps(KB)
    tap_high = tap.astype(ml_dtypes.bfloat16)
    tap_low = (tap - tap_high.astype(np.float32)).astype(ml_dtypes.bfloat16)
    vmem = pl.BlockSpec(memory_space=pltpu.VMEM)
    return pl.pallas_call(
        filter_kernel,
        out_shape=jax.ShapeDtypeStruct((rows, 2 * channels), BF),
        in_specs=[vmem] * 5,
        out_specs=vmem,
        scratch_shapes=[pltpu.VMEM((rows, 2 * channels - KB + 4 * KB), BF)] * 2,
        compiler_params=pltpu.CompilerParams(vmem_limit_bytes=56 * 2**20),
        name="filter",
    )(got.reshape(parts, kinds, owners * slots, chunk), sums, jnp.asarray(tap_high), jnp.asarray(tap_low), feather)


def ranked(owner, owners):
    rows = owner.shape[-1]
    onehot = (owner[..., None] == jnp.arange(owners)).astype(BF)
    earlier = (jnp.arange(rows)[:, None] > jnp.arange(rows)[None, :]).astype(BF)
    before = jnp.einsum("rk,...ko->...ro", earlier, onehot, preferred_element_type=F32)
    return jnp.sum(before * onehot.astype(F32), -1).astype(jnp.int32)


def local(projections, partner_view, row_weight, row_slab):
    blocks, owners = lax.axis_size("angle"), lax.axis_size("gz")
    views, rows_dev, channels = projections.shape
    rows = views * rows_dev
    capacity = 2 * rows // owners
    slots = -(-capacity // 16) * 16
    half = blocks // 2
    other_slab = lax.ppermute(row_slab, "angle", [(s, (s + half) % blocks) for s in range(blocks)])
    meta = lax.all_gather(
        jnp.concatenate([row_slab.astype(F32), row_weight.astype(F32)], 0), "gz", axis=0
    )

    def slot_of(slab):
        owner = slab.reshape(rows) // SLAB_DEV
        return owner * slots + ranked(owner, owners)

    own_slot = slot_of(row_slab)
    other_slot = slot_of(other_slab).reshape(views, rows_dev)
    local_partner = partner_view % views
    is_partner = (local_partner[:, None] == jnp.arange(views)[None, :]).astype(jnp.int32)
    mirror_slot = jnp.sum(is_partner[:, :, None] * other_slot[None], 1).reshape(rows)
    slot_list = jnp.arange(owners * slots)[:, None]
    pick_own = (own_slot[None, :] == slot_list).astype(BF)
    pick_mirror = (mirror_slot[None, :] == slot_list).astype(BF)
    flip = (jnp.arange(KB)[:, None] + jnp.arange(KB)[None, :] == KB - 1).astype(BF)
    got = exchange(
        projections.reshape(rows, channels), pick_own, pick_mirror, flip, owners, blocks, slots
    )

    all_slab = meta[:, :views].reshape(owners, rows).astype(jnp.int32)
    all_weight = meta[:, views:].reshape(owners, rows).astype(BF)
    owner = all_slab // SLAB_DEV
    slot = jnp.where(owner == lax.axis_index("gz"), ranked(owner, owners), -1)
    target = jnp.arange(rows) // rows_dev * SLAB_DEV + all_slab % SLAB_DEV
    goes = jnp.where(
        target[:, None, :] == jnp.arange(views * SLAB_DEV)[:, None], all_weight[:, None, :], 0
    ).astype(BF)
    stands = (slot[:, :, None] == jnp.arange(slots)).astype(BF)
    sums = jnp.einsum("gtr,grs->tgs", goes, stands, preferred_element_type=F32)
    sums = sums.astype(BF).reshape(views * SLAB_DEV, owners * slots)
    ramp_part = np.clip((np.arange(KB) + 0.5) / (2.0 * OV), 0.0, 1.0)
    feather = jnp.asarray((np.sin(0.5 * math.pi * ramp_part) ** 2)[None, :], F32)
    return filtered_slabs(got, sums, feather).reshape(views, SLAB_DEV, 2 * channels)


def solution(mesh):
    in_specs = (P("angle", "gz", None), P("angle"), P("angle", "gz"), P("angle", "gz"))
    out_specs = P("angle", "gz", None)
    return jax.shard_map(local, mesh=mesh, in_specs=in_specs, out_specs=out_specs, check_vma=False)
```

profile of v0, /device:TPU:0, one launch (start us, length us, event | category | flops | bytes accessed | tf_op | source)
XLA Modules:
  0.0 193.5 jit_solution(16949554283831583519)
XLA Ops:
  0.0 2.9 %collective-permute-start = (s32[12,16]{1,0:T(8,128)}, s32[12,16]{1,0:T(8,128)S(1)}, u32[]{:S(2)}, u32[]{:S(2)}) collective-permute-start(s32[12,16]{1,0:T(8,128)} %param.10), channel_id=1, source_target_pairs={{0,16},{8,24},{16,0},{24,8},{1,17},{9,25},{17,1},{25,9},{2,18},{10... | collective-permute-start | bytes 2312 | tf_op jit(solution)/shard_map/ppermute | solution.py:185
  2.9 0.8 reshape.233
  3.8 0.8 copy.20
  4.5 0.7 and_select_fusion.2
  5.2 0.2 fusion.3
  5.4 0.8 copy.21
  6.2 0.1 fusion.23
  6.3 0.1 maximum_bitcast_fusion
  6.3 30.8 %all-gather.1 = f32[8,24,16]{1,2,0:T(8,128)S(1)} all-gather(f32[1,24,16]{1,2,0:T(8,128)S(1)} %maximum_bitcast_fusion), channel_id=2, replica_groups=mesh['angle'=4,'gz'=8] {'gz'}, dimensions={0}, use_global_device_ids=true | all-gather | bytes 13824 | tf_op jit(solution)/shard_map/all_gather | solution.py:186
  37.2 0.1 slice.12
  37.3 0.0 copy-start
  37.3 0.1 copy.24
  37.4 0.1 convert_element_type.117
  37.5 0.1 copy.26
  37.7 0.1 convert_element_type.113
  37.8 0.2 fusion.2
  38.0 0.4 convolution_convert_fusion
  38.4 0.8 copy.25.sum_ref
  39.2 0.0 collective-permute-done
  39.2 0.1 reshape.234
  39.3 0.2 fusion.4
  39.4 0.1 convert_element_type.107
  39.6 0.1 multiply_reduce_fusion
  39.7 0.1 eq.142
  39.7 0.1 fusion.9
  39.9 0.0 copy-done
  39.9 139.6 %exchange.1 = bf16[2,2,8,48,2048]{4,3,2,1,0:T(8,128)(2,1)} custom-call(bf16[192,4096]{1,0:T(8,128)(2,1)S(1)} %bitcast.18, bf16[384,192]{1,0:T(8,128)(2,1)S(1)} %get-tuple-element.7.pick_own_ref, bf16[384,192]{1,0:T(8,128)(2,1)S(1)} %get-tuple-element.8.pick_mirror_ref, bf16[256,256]{1,0:T(8,128)(2,1)S(1)} %fusion.11.flip_ref), custom_call_target="tpu_custom_call" | custom-call | tf_op jit(solution)/shard_map/exchange/pallas_call | solution.py:90
  179.5 14.0 %filter.1 = bf16[192,8192]{1,0:T(8,128)(2,1)} custom-call(bf16[2,2,384,2048]{3,2,1,0:T(8,128)(2,1)} %bitcast.19, bf16[192,384]{1,0:T(8,128)(2,1)} %copy.25.sum_ref, bf16[768,256]{1,0:T(8,128)(2,1)} %constant.86.clone.high_ref, bf16[768,256]{1,0:T(8,128)(2,1)} %constant.87.clone.low_ref, f32[1,256]{1,0:T(1,128)} %constant.85.clone.feather_ref), custom_call_target="tpu_custom_call" | custom-call | tf_op jit(solution)/shard_map/filter/pallas_call | solution.py:159
  (13 shorter events, 0.2 us)
Async XLA Ops:
  0.0 39.2 %collective-permute-start = (s32[12,16]{1,0:T(8,128)}, s32[12,16]{1,0:T(8,128)S(1)}, u32[]{:S(2)}, u32[]{:S(2)}) collective-permute-start(s32[12,16]{1,0:T(8,128)} %param.10), channel_id=1, source_target_pairs={{0,16},{8,24},{16,0},{24,8},{1,17},{9,25},{17,1},{25,9},{2,18},{10... | collective-permute-start | bytes 2312 | tf_op jit(solution)/shard_map/ppermute | solution.py:185
  37.3 2.6 %copy-start = (bf16[12,16,4096]{2,1,0:T(8,128)(2,1)S(1)}, bf16[12,16,4096]{2,1,0:T(8,128)(2,1)}, u32[]{:S(2)}) copy-start(bf16[12,16,4096]{2,1,0:T(8,128)(2,1)} %param.7) | copy-start | bytes 4718596
where the time goes:
time: 194 us
  Pallas kernels  154 us (79%)
  blocking collectives  30.8 us (16%)
  local copies, waits for them, and re-layouts  3.89 us (2%)
  starting transfers between devices  2.94 us (2%)
    pallas_call x1, Pallas kernels, exchange(): pl.pallas_call(functools.partial(exchange_kernel, owners, blocks, chunk),...  140 us
    all_gather x1, blocking collectives, local(): lax.all_gather(jnp.concatenate([row_slab.astype(F32), row_weight.astype(F...  30.8 us
    pallas_call x1, Pallas kernels, filtered_slabs(): pl.pallas_call(filter_kernel, out_shape=jax.ShapeDtypeStruct((rows, 2 * c...  14 us
  transfers between devices with their start and end apart: 1, of which 0 were waited for; matrix products, arithmetic and copies ran while one was open for 3% of the time, Pallas kernels for 0%

commit v1 on v0

--- a/solution.py
+++ b/solution.py
@@ -29,8 +29,8 @@
 
 
 def exchange_kernel(
-    owners, blocks, chunk, raw_ref, pick_own_ref, pick_mirror_ref, flip_ref, got_ref,
-    flipped, outgoing, send_sem, recv_sem, local_sem,
+    owners, blocks, chunk, raw_ref, pick_own_ref, pick_mirror_ref, flip_ref, lists_ref, got_ref,
+    got_lists_ref, flipped, outgoing, send_sem, recv_sem, local_sem, lists_send, lists_recv,
 ):
     me_a, me_g = lax.axis_index("angle"), lax.axis_index("gz")
     partner = lax.rem(me_a + blocks // 2, blocks)
@@ -51,6 +51,20 @@
         flipped[:, to:to + KB] = block.astype(BF)
     pl.semaphore_wait(barrier, 2 * owners - 1)
     copies = []
+    for step in range(owners):
+        if step == 0:
+            copy = pltpu.make_async_copy(lists_ref, got_lists_ref.at[me_g], lists_send.at[0])
+        else:
+            copy = pltpu.make_async_remote_copy(
+                src_ref=lists_ref,
+                dst_ref=got_lists_ref.at[me_g],
+                send_sem=lists_send.at[step],
+                recv_sem=lists_recv.at[step],
+                device_id=(me_a, lax.rem(me_g + step, owners)),
+                device_id_type=MESH,
+            )
+        copy.start()
+        copies.append(copy)
     for part in range(channels // chunk):
         for kind in range(2):
             pick = pick_own_ref if kind == 0 else pick_mirror_ref
@@ -83,27 +97,32 @@
         copy.wait()
 
 
-def exchange(raw, pick_own, pick_mirror, flip, owners, blocks, slots):
+def exchange(raw, pick_own, pick_mirror, flip, lists, owners, blocks, slots):
     rows, channels = raw.shape
     chunk = channels // CHUNKS
     vmem = pl.BlockSpec(memory_space=pltpu.VMEM)
     return pl.pallas_call(
         functools.partial(exchange_kernel, owners, blocks, chunk),
-        out_shape=jax.ShapeDtypeStruct((CHUNKS, 2, owners, slots, chunk), BF),
-        in_specs=[vmem] * 4,
-        out_specs=pl.BlockSpec(memory_space=pl.ANY),
+        out_shape=[
+            jax.ShapeDtypeStruct((CHUNKS, 2, owners, slots, chunk), BF),
+            jax.ShapeDtypeStruct((owners,) + lists.shape, F32),
+        ],
+        in_specs=[vmem] * 5,
+        out_specs=[pl.BlockSpec(memory_space=pl.ANY)] * 2,
         scratch_shapes=[
             pltpu.VMEM((rows, channels), BF),
             pltpu.VMEM((CHUNKS, 2, owners, slots, chunk), BF),
             pltpu.SemaphoreType.DMA((CHUNKS, 2, owners)),
             pltpu.SemaphoreType.DMA((CHUNKS, 2, owners)),
             pltpu.SemaphoreType.DMA((CHUNKS,)),
+            pltpu.SemaphoreType.DMA((owners,)),
+            pltpu.SemaphoreType.DMA((owners,)),
         ],
         compiler_params=pltpu.CompilerParams(
             collective_id=0, has_side_effects=True, vmem_limit_bytes=48 * 2**20
         ),
         name="exchange",
-    )(raw, pick_own, pick_mirror, flip)
+    )(raw, pick_own, pick_mirror, flip, lists)
 
 
 def filter_kernel(got_ref, sum_ref, high_ref, low_ref, feather_ref, out_ref, high, low):
@@ -183,9 +202,8 @@
     slots = -(-capacity // 16) * 16
     half = blocks // 2
     other_slab = lax.ppermute(row_slab, "angle", [(s, (s + half) % blocks) for s in range(blocks)])
-    meta = lax.all_gather(
-        jnp.concatenate([row_slab.astype(F32), row_weight.astype(F32)], 0), "gz", axis=0
-    )
+    lists = jnp.concatenate([row_slab.astype(F32), row_weight.astype(F32)], 0)
+    lists = jnp.pad(lists, ((0, 0), (0, 128 - rows_dev)))
 
     def slot_of(slab):
         owner = slab.reshape(rows) // SLAB_DEV
@@ -200,9 +218,11 @@
     pick_own = (own_slot[None, :] == slot_list).astype(BF)
     pick_mirror = (mirror_slot[None, :] == slot_list).astype(BF)
     flip = (jnp.arange(KB)[:, None] + jnp.arange(KB)[None, :] == KB - 1).astype(BF)
-    got = exchange(
-        projections.reshape(rows, channels), pick_own, pick_mirror, flip, owners, blocks, slots
+    got, meta = exchange(
+        projections.reshape(rows, channels), pick_own, pick_mirror, flip, lists, owners, blocks,
+        slots,
     )
+    meta = meta[:, :, :rows_dev]
 
     all_slab = meta[:, :views].reshape(owners, rows).astype(jnp.int32)
     all_weight = meta[:, views:].reshape(owners, rows).astype(BF)

time: 194 us -> 172 us (0.89)
  blocking collectives: 30.8 us -> 0 us
  Pallas kernels: 154 us -> 161 us
    all_gather x1 -> x0, blocking collectives: 30.8 us -> none  [local(): lax.all_gather(jnp.concatenate([row_slab.astype(F32), row_weight.astype(F...]
    pallas_call x1, Pallas kernels: 140 us -> 147 us  [exchange(): pl.pallas_call(functools.partial(exchange_kernel, owners, blocks, chunk),...]
  transfers between devices with their start and end apart: 1 -> 1, of which waited for: 0 -> 0; matrix products, arithmetic and copies ran while one was open for 3% -> 2% of each run, Pallas kernels for 0% -> 0%
where the time goes in v1:
time: 172 us; the launch traced here: 171 us
  Pallas kernels  161 us (94%)
  local copies, waits for them, and re-layouts  3.41 us (2%)
  starting transfers between devices  2.94 us (2%)
  other arithmetic  2.51 us (1%)
    pallas_call x1, Pallas kernels, exchange(): pl.pallas_call(functools.partial(exchange_kernel, owners, blocks, chunk),...  147 us
    pallas_call x1, Pallas kernels, filtered_slabs(): pl.pallas_call(filter_kernel, out_shape=jax.ShapeDtypeStruct((rows, 2 * c...  14 us
  transfers between devices with their start and end apart: 1, of which 0 were waited for; matrix products, arithmetic and copies ran while one was open for 2% of the time, Pallas kernels for 0%

profile of v1, /device:TPU:0, one launch (start us, length us, event | category | flops | bytes accessed | tf_op | source)
XLA Modules:
  0.0 171.3 jit_solution(13279081466391217459)
XLA Ops:
  0.0 2.9 %collective-permute-start = (s32[12,16]{1,0:T(8,128)}, s32[12,16]{1,0:T(8,128)S(1)}, u32[]{:S(2)}, u32[]{:S(2)}) collective-permute-start(s32[12,16]{1,0:T(8,128)} %param.10), channel_id=1, source_target_pairs={{0,16},{8,24},{16,0},{24,8},{1,17},{9,25},{17,1},{25,9},{2,18},{10... | collective-permute-start | bytes 2312 | tf_op jit(solution)/shard_map/ppermute | solution.py:204
  2.9 0.8 reshape.233
  3.7 0.7 convert_element_type.112
  4.5 0.7 and_select_fusion.2
  5.2 0.2 fusion.3
  5.4 0.1 fusion.23
  5.4 0.7 convert_element_type.113
  6.1 0.0 collective-permute-done
  6.2 0.1 reshape.234
  6.3 0.2 fusion.4
  6.4 0.1 convert_element_type.109
  6.5 0.1 multiply_reduce_fusion
  6.7 0.1 eq.142
  6.7 0.1 fusion.9
  6.8 0.0 copy-start
  6.9 1.4 copy-done
  8.3 147.5 %exchange.1 = (bf16[2,2,8,48,2048]{4,3,2,1,0:T(8,128)(2,1)}, f32[8,24,128]{2,1,0:T(8,128)S(1)}) custom-call(bf16[192,4096]{1,0:T(8,128)(2,1)S(1)} %bitcast.15, bf16[384,192]{1,0:T(8,128)(2,1)S(1)} %get-tuple-element.11.pick_own_ref, bf16[384,192]{1,0:T(8,128)(2,1)S(1)} %get-tuple-element.12.pick_mirror_ref, bf16[256,256]{1,0:T(8,128)(2,1)S(1)} %fusion.11.flip_ref, ...), custom_call_target="tpu_custom_call" | custom-call | tf_op jit(solution)/shard_map/exchange/pallas_call | solution.py:104
  155.8 0.1 convert_element_type.115
  155.9 0.1 convert_element_type.119
  156.0 0.2 fusion.2
  156.2 0.4 convolution_convert_fusion
  156.5 0.8 copy.10.sum_ref
  157.3 14.0 %filter.1 = bf16[192,8192]{1,0:T(8,128)(2,1)} custom-call(bf16[2,2,384,2048]{3,2,1,0:T(8,128)(2,1)} %bitcast.16, bf16[192,384]{1,0:T(8,128)(2,1)} %copy.10.sum_ref, bf16[768,256]{1,0:T(8,128)(2,1)} %constant.87.clone.high_ref, bf16[768,256]{1,0:T(8,128)(2,1)} %constant.88.clone.low_ref, f32[1,256]{1,0:T(1,128)} %constant.86.clone.feather_ref), custom_call_target="tpu_custom_call" | custom-call | tf_op jit(solution)/shard_map/filter/pallas_call | solution.py:178
  (12 shorter events, 0.2 us)
Async XLA Ops:
  0.0 6.2 %collective-permute-start = (s32[12,16]{1,0:T(8,128)}, s32[12,16]{1,0:T(8,128)S(1)}, u32[]{:S(2)}, u32[]{:S(2)}) collective-permute-start(s32[12,16]{1,0:T(8,128)} %param.10), channel_id=1, source_target_pairs={{0,16},{8,24},{16,0},{24,8},{1,17},{9,25},{17,1},{25,9},{2,18},{10... | collective-permute-start | bytes 2312 | tf_op jit(solution)/shard_map/ppermute | solution.py:204
  6.8 1.4 copy-start

commit v2 on v1

--- a/solution.py
+++ b/solution.py
@@ -13,7 +13,7 @@
 OV = 128
 KB = 256
 SLAB_DEV = 16
-CHUNKS = 2
+CHUNKS = 4
 BF = jnp.bfloat16
 F32 = jnp.float32
 MESH = pl.DeviceIdType.MESH
@@ -29,28 +29,40 @@
 
 
 def exchange_kernel(
-    owners, blocks, chunk, raw_ref, pick_own_ref, pick_mirror_ref, flip_ref, lists_ref, got_ref,
-    got_lists_ref, flipped, outgoing, send_sem, recv_sem, local_sem, lists_send, lists_recv,
+    owners, blocks, chunk, raw_ref, pick_ref, flip_ref, lists_ref, got_ref, got_lists_ref, far,
+    flipped, outgoing, send_sem, recv_sem, local_sem, far_send, far_recv, lists_send, lists_recv,
 ):
     me_a, me_g = lax.axis_index("angle"), lax.axis_index("gz")
     partner = lax.rem(me_a + blocks // 2, blocks)
-    slots = outgoing.shape[3]
-    channels = raw_ref.shape[1]
+    half = owners // 2
+    base = me_g // half * half
+    place = me_g - base
+    far_g = lax.rem(me_g + half, owners)
+    slots = outgoing.shape[4]
+    parts = raw_ref.shape[1] // chunk
     barrier = pltpu.get_barrier_semaphore()
-    for kind in range(2):
-        target_a = me_a if kind == 0 else partner
-        for step in range(1 - kind, owners):
-            pl.semaphore_signal(
-                barrier, inc=1, device_id=(target_a, lax.rem(me_g + step, owners)),
-                device_id_type=MESH,
-            )
-    width = 2 * KB
-    for at in range(channels // KB):
-        block = jnp.dot(raw_ref[:, at * KB:(at + 1) * KB], flip_ref[...], preferred_element_type=F32)
-        to = channels - (at + 1) * KB
-        flipped[:, to:to + KB] = block.astype(BF)
-    pl.semaphore_wait(barrier, 2 * owners - 1)
-    copies = []
+    for step in range(1, owners):
+        pl.semaphore_signal(
+            barrier, inc=1, device_id=(me_a, lax.rem(me_g + step, owners)), device_id_type=MESH
+        )
+    for step in range(half):
+        pl.semaphore_signal(
+            barrier, inc=1, device_id=(partner, base + lax.rem(place + step, half)),
+            device_id_type=MESH,
+        )
+    pl.semaphore_wait(barrier, owners - 1 + half)
+    copies, crossing = [], []
+    for part in range(parts):
+        copy = pltpu.make_async_remote_copy(
+            src_ref=raw_ref.at[:, part * chunk:(part + 1) * chunk],
+            dst_ref=far.at[part],
+            send_sem=far_send.at[part],
+            recv_sem=far_recv.at[part],
+            device_id=(me_a, far_g),
+            device_id_type=MESH,
+        )
+        copy.start()
+        crossing.append(copy)
     for step in range(owners):
         if step == 0:
             copy = pltpu.make_async_copy(lists_ref, got_lists_ref.at[me_g], lists_send.at[0])
@@ -65,39 +77,57 @@
             )
         copy.start()
         copies.append(copy)
-    for part in range(channels // chunk):
-        for kind in range(2):
-            pick = pick_own_ref if kind == 0 else pick_mirror_ref
-            source = raw_ref if kind == 0 else flipped
-            for at in range(chunk // width):
-                begin = part * chunk + at * width
-                rows = jnp.dot(pick[...], source[:, begin:begin + width], preferred_element_type=F32)
-                rows = rows.astype(BF).reshape(owners, slots, width)
-                outgoing[part, kind, :, :, at * width:(at + 1) * width] = rows
-            target_a = me_a if kind == 0 else partner
-            for step in range(owners - 1, -1, -1):
-                to = lax.rem(me_g + step, owners)
-                if kind == 0 and step == 0:
-                    copy = pltpu.make_async_copy(
-                        outgoing.at[part, kind, me_g], got_ref.at[part, kind, me_g],
-                        local_sem.at[part],
+    width = 2 * KB
+    for origin in range(2):
+        source_g = me_g if origin == 0 else far_g
+        for part in range(parts):
+            if origin == 1:
+                crossing[part].wait()
+            for at in range(chunk // KB):
+                begin = part * chunk + at * KB
+                block = (
+                    raw_ref[:, begin:begin + KB] if origin == 0
+                    else far[part, :, at * KB:(at + 1) * KB]
+                )
+                block = jnp.dot(block, flip_ref[...], preferred_element_type=F32)
+                to = chunk - (at + 1) * KB
+                flipped[:, to:to + KB] = block.astype(BF)
+            for kind in range(2):
+                out_part = part if kind == 0 else parts - 1 - part
+                for at in range(0, chunk, width):
+                    if kind == 1:
+                        block = flipped[:, at:at + width]
+                    elif origin == 0:
+                        block = raw_ref[:, part * chunk + at:part * chunk + at + width]
+                    else:
+                        block = far[part, :, at:at + width]
+                    rows = jnp.dot(pick_ref[origin, kind], block, preferred_element_type=F32)
+                    outgoing[out_part, kind, origin, :, :, at:at + width] = (
+                        rows.astype(BF).reshape(half, slots, width)
                     )
-                else:
-                    copy = pltpu.make_async_remote_copy(
-                        src_ref=outgoing.at[part, kind, to],
-                        dst_ref=got_ref.at[part, kind, me_g],
-                        send_sem=send_sem.at[part, kind, step],
-                        recv_sem=recv_sem.at[part, kind, step],
-                        device_id=(target_a, to),
-                        device_id_type=MESH,
-                    )
-                copy.start()
-                copies.append(copy)
+                target_a = me_a if kind == 0 else partner
+                for step in range(half - 1, -1, -1):
+                    to = lax.rem(place + step, half)
+                    source = outgoing.at[out_part, kind, origin, to]
+                    target = got_ref.at[out_part, kind, source_g]
+                    if kind == 0 and step == 0:
+                        copy = pltpu.make_async_copy(source, target, local_sem.at[part, origin])
+                    else:
+                        copy = pltpu.make_async_remote_copy(
+                            src_ref=source,
+                            dst_ref=target,
+                            send_sem=send_sem.at[out_part, kind, origin, step],
+                            recv_sem=recv_sem.at[out_part, kind, origin, step],
+                            device_id=(target_a, base + to),
+                            device_id_type=MESH,
+                        )
+                    copy.start()
+                    copies.append(copy)
     for copy in copies:
         copy.wait()
 
 
-def exchange(raw, pick_own, pick_mirror, flip, lists, owners, blocks, slots):
+def exchange(raw, pick, flip, lists, owners, blocks, slots):
     rows, channels = raw.shape
     chunk = channels // CHUNKS
     vmem = pl.BlockSpec(memory_space=pltpu.VMEM)
@@ -107,13 +137,16 @@
             jax.ShapeDtypeStruct((CHUNKS, 2, owners, slots, chunk), BF),
             jax.ShapeDtypeStruct((owners,) + lists.shape, F32),
         ],
-        in_specs=[vmem] * 5,
+        in_specs=[vmem] * 4,
         out_specs=[pl.BlockSpec(memory_space=pl.ANY)] * 2,
         scratch_shapes=[
-            pltpu.VMEM((rows, channels), BF),
-            pltpu.VMEM((CHUNKS, 2, owners, slots, chunk), BF),
-            pltpu.SemaphoreType.DMA((CHUNKS, 2, owners)),
-            pltpu.SemaphoreType.DMA((CHUNKS, 2, owners)),
+            pltpu.VMEM((CHUNKS, rows, chunk), BF),
+            pltpu.VMEM((rows, chunk), BF),
+            pltpu.VMEM((CHUNKS, 2, 2, owners // 2, slots, chunk), BF),
+            pltpu.SemaphoreType.DMA((CHUNKS, 2, 2, owners // 2)),
+            pltpu.SemaphoreType.DMA((CHUNKS, 2, 2, owners // 2)),
+            pltpu.SemaphoreType.DMA((CHUNKS, 2)),
+            pltpu.SemaphoreType.DMA((CHUNKS,)),
             pltpu.SemaphoreType.DMA((CHUNKS,)),
             pltpu.SemaphoreType.DMA((owners,)),
             pltpu.SemaphoreType.DMA((owners,)),
@@ -122,7 +155,7 @@
             collective_id=0, has_side_effects=True, vmem_limit_bytes=48 * 2**20
         ),
         name="exchange",
-    )(raw, pick_own, pick_mirror, flip, lists)
+    )(raw, pick, flip, lists)
 
 
 def filter_kernel(got_ref, sum_ref, high_ref, low_ref, feather_ref, out_ref, high, low):
@@ -209,18 +242,23 @@
         owner = slab.reshape(rows) // SLAB_DEV
         return owner * slots + ranked(owner, owners)
 
-    own_slot = slot_of(row_slab)
-    other_slot = slot_of(other_slab).reshape(views, rows_dev)
+    pair = jnp.stack([row_slab, other_slab])
+    far = owners // 2
+    far_pair = lax.ppermute(pair, "gz", [(s, (s + far) % owners) for s in range(owners)])
     local_partner = partner_view % views
     is_partner = (local_partner[:, None] == jnp.arange(views)[None, :]).astype(jnp.int32)
-    mirror_slot = jnp.sum(is_partner[:, :, None] * other_slot[None], 1).reshape(rows)
-    slot_list = jnp.arange(owners * slots)[:, None]
-    pick_own = (own_slot[None, :] == slot_list).astype(BF)
-    pick_mirror = (mirror_slot[None, :] == slot_list).astype(BF)
+    slot_list = (lax.axis_index("gz") // far * far * slots + jnp.arange(far * slots))[:, None]
+
+    def picks(own_slab, partner_slab):
+        own_slot = slot_of(own_slab)
+        other_slot = slot_of(partner_slab).reshape(views, rows_dev)
+        mirror_slot = jnp.sum(is_partner[:, :, None] * other_slot[None], 1).reshape(rows)
+        return jnp.stack([own_slot[None, :] == slot_list, mirror_slot[None, :] == slot_list])
+
+    pick = jnp.stack([picks(pair[0], pair[1]), picks(far_pair[0], far_pair[1])]).astype(BF)
     flip = (jnp.arange(KB)[:, None] + jnp.arange(KB)[None, :] == KB - 1).astype(BF)
     got, meta = exchange(
-        projections.reshape(rows, channels), pick_own, pick_mirror, flip, lists, owners, blocks,
-        slots,
+        projections.reshape(rows, channels), pick, flip, lists, owners, blocks, slots
     )
     meta = meta[:, :, :rows_dev]
 

time: 172 us -> 140 us (0.81)
  Pallas kernels: 161 us -> 125 us
  starting transfers between devices: 2.94 us -> 5.53 us
  waiting for transfers between devices: 0.01 us -> 2.04 us
    pallas_call x1, Pallas kernels: 147 us -> 111 us  [exchange(): pl.pallas_call(functools.partial(exchange_kernel, owners, blocks, chunk),...]
    ppermute x0 -> x1, starting transfers between devices: none -> 2.59 us  [local(): lax.ppermute(pair, 'gz', [(s, (s + far) % owners) for s in range(owners)])]
    ppermute x0 -> x1, waiting for transfers between devices: none -> 2.04 us  [local(): lax.ppermute(pair, 'gz', [(s, (s + far) % owners) for s in range(owners)])]
  transfers between devices with their start and end apart: 1 -> 2, of which waited for: 0 -> 1; matrix products, arithmetic and copies ran while one was open for 2% -> 2% of each run, Pallas kernels for 0% -> 0%
where the time goes in v2:
time: 140 us; the launch traced here: 139 us
  Pallas kernels  125 us (89%)
  starting transfers between devices  5.53 us (4%)
  other arithmetic  3.58 us (3%)
  local copies, waits for them, and re-layouts  2.33 us (2%)
  waiting for transfers between devices  2.04 us (1%)
    pallas_call x1, Pallas kernels, exchange(): pl.pallas_call(functools.partial(exchange_kernel, owners, blocks, chunk),...  111 us
    pallas_call x1, Pallas kernels, filtered_slabs(): pl.pallas_call(filter_kernel, out_shape=jax.ShapeDtypeStruct((rows, 2 * c...  14 us
    ppermute x1, starting transfers between devices, local(): lax.ppermute(row_slab, 'angle', [(s, (s + half) % blocks) for s in range(...  2.94 us
  transfers between devices with their start and end apart: 2, of which 1 were waited for; matrix products, arithmetic and copies ran while one was open for 2% of the time, Pallas kernels for 0%

profile of v2, /device:TPU:0, one launch (start us, length us, event | category | flops | bytes accessed | tf_op | source)
XLA Modules:
  0.0 139.4 jit_solution(6787765348609852178)
XLA Ops:
  0.0 0.0 copy-start
  0.0 2.9 %collective-permute-start = (s32[12,16]{1,0:T(8,128)}, s32[12,16]{1,0:T(8,128)S(1)}, u32[]{:S(2)}, u32[]{:S(2)}) collective-permute-start(s32[12,16]{1,0:T(8,128)} %param.10), channel_id=1, source_target_pairs={{0,16},{8,24},{16,0},{24,8},{1,17},{9,25},{17,1},{25,9},{2,18},{10... | collective-permute-start | bytes 2312 | tf_op jit(solution)/shard_map/ppermute | solution.py:237
  2.9 0.8 reshape_squeeze_stack.8
  3.8 0.7 convert_element_type.149
  4.5 0.7 and_select_fusion.4
  5.2 0.2 fusion.3
  5.4 0.1 fusion.29
  5.4 0.7 convert_element_type.150
  6.2 0.0 collective-permute-done
  6.2 0.1 reshape_squeeze_stack.9
  6.3 0.2 fusion.4
  6.5 0.1 convert_element_type.139
  6.5 0.7 pad_add_fusion
  7.2 2.6 %collective-permute-start.1 = (s32[2,12,16]{2,1,0:T(8,128)S(1)}, s32[2,12,16]{2,1,0:T(8,128)S(1)}, u32[]{:S(2)}, u32[]{:S(2)}) collective-permute-start(s32[2,12,16]{2,1,0:T(8,128)S(1)} %pad_add_fusion), channel_id=1, source_target_pairs={{0,4},{1,5},{2,6},{3,7},{4,0},{5,1},{6,2},{7,3},{8,12},{9,13},{10,... | collective-permute-start | bytes 4616 | tf_op jit(solution)/shard_map/ppermute | solution.py:247
  9.8 2.0 %collective-permute-done.1 = s32[2,12,16]{2,1,0:T(8,128)S(1)} collective-permute-done((s32[2,12,16]{2,1,0:T(8,128)S(1)}, s32[2,12,16]{2,1,0:T(8,128)S(1)}, u32[]{:S(2)}, u32[]{:S(2)}) %collective-permute-start.1) | collective-permute-done | bytes 1568 | tf_op jit(solution)/shard_map/ppermute | solution.py:247
  11.9 0.1 reshape_squeeze.7
  12.0 0.2 fusion.6
  12.2 0.1 convert_element_type.146
  12.3 0.1 reshape_squeeze.6
  12.4 0.1 multiply_reduce_fusion.1
  12.5 0.1 eq.218
  12.6 0.1 eq.229
  12.7 0.2 fusion.5
  12.9 0.2 broadcast_compare_fusion.3
  13.0 0.1 add_bitcast_fusion
  13.1 0.1 add_convert_fusion.pick_ref
  13.2 0.0 copy-done
  13.2 110.5 %exchange.1 = (bf16[4,2,8,48,1024]{4,3,2,1,0:T(8,128)(2,1)}, f32[8,24,128]{2,1,0:T(8,128)S(1)}) custom-call(bf16[192,4096]{1,0:T(8,128)(2,1)S(1)} %bitcast.23, bf16[2,2,192,192]{3,2,1,0:T(8,128)(2,1)S(1)} %add_convert_fusion.pick_ref, bf16[256,256]{1,0:T(8,128)(2,1)S(1)} %fusion.11.flip_ref, f32[24,128]{1,0:T(8,128)S(1)} %select_maximum_fusion.lists_ref), custom_call_target="tpu_custom_call" | custom-call | tf_op jit(solution)/shard_map/exchange/pallas_call | solution.py:134
  123.8 0.1 convert_element_type.152
  123.9 0.1 convert_element_type.156
  124.0 0.2 fusion.2
  124.2 0.4 convolution_convert_fusion
  124.6 0.8 copy.10.sum_ref
  125.4 14.0 %filter.1 = bf16[192,8192]{1,0:T(8,128)(2,1)} custom-call(bf16[4,2,384,1024]{3,2,1,0:T(8,128)(2,1)} %bitcast.24, bf16[192,384]{1,0:T(8,128)(2,1)} %copy.10.sum_ref, bf16[768,256]{1,0:T(8,128)(2,1)} %constant.117.clone.high_ref, bf16[768,256]{1,0:T(8,128)(2,1)} %constant.118.clone.low_ref, f32[1,256]{1,0:T(1,128)} %constant.116.clone.feather_ref), custom_call_target="tpu_custom_call" | custom-call | tf_op jit(solution)/shard_map/filter/pallas_call | solution.py:211
  (19 shorter events, 0.3 us)
Async XLA Ops:
  0.0 13.2 %copy-start = (bf16[12,16,4096]{2,1,0:T(8,128)(2,1)S(1)}, bf16[12,16,4096]{2,1,0:T(8,128)(2,1)}, u32[]{:S(2)}) copy-start(bf16[12,16,4096]{2,1,0:T(8,128)(2,1)} %param.7) | copy-start | bytes 4718596
  0.0 6.2 %collective-permute-start = (s32[12,16]{1,0:T(8,128)}, s32[12,16]{1,0:T(8,128)S(1)}, u32[]{:S(2)}, u32[]{:S(2)}) collective-permute-start(s32[12,16]{1,0:T(8,128)} %param.10), channel_id=1, source_target_pairs={{0,16},{8,24},{16,0},{24,8},{1,17},{9,25},{17,1},{25,9},{2,18},{10... | collective-permute-start | bytes 2312 | tf_op jit(solution)/shard_map/ppermute | solution.py:237
  7.2 4.6 %collective-permute-start.1 = (s32[2,12,16]{2,1,0:T(8,128)S(1)}, s32[2,12,16]{2,1,0:T(8,128)S(1)}, u32[]{:S(2)}, u32[]{:S(2)}) collective-permute-start(s32[2,12,16]{2,1,0:T(8,128)S(1)} %pad_add_fusion), channel_id=1, source_target_pairs={{0,4},{1,5},{2,6},{3,7},{4,0},{5,1},{6,2},{7,3},{8,12},{9,13},{10,... | collective-permute-start | bytes 4616 | tf_op jit(solution)/shard_map/ppermute | solution.py:247

commit v3 on v2

--- a/solution.py
+++ b/solution.py
@@ -29,8 +29,9 @@
 
 
 def exchange_kernel(
-    owners, blocks, chunk, raw_ref, pick_ref, flip_ref, lists_ref, got_ref, got_lists_ref, far,
-    flipped, outgoing, send_sem, recv_sem, local_sem, far_send, far_recv, lists_send, lists_recv,
+    owners, blocks, chunk, raw_ref, swap_ref, flip_ref, lists_ref, got_ref, got_lists_ref, far,
+    flipped, outgoing, near, pick_ref, send_sem, recv_sem, local_sem, far_send, far_recv,
+    lists_send, lists_recv, near_send, near_recv,
 ):
     me_a, me_g = lax.axis_index("angle"), lax.axis_index("gz")
     partner = lax.rem(me_a + blocks // 2, blocks)
@@ -50,7 +51,20 @@
             barrier, inc=1, device_id=(partner, base + lax.rem(place + step, half)),
             device_id_type=MESH,
         )
-    pl.semaphore_wait(barrier, owners - 1 + half)
+    pl.semaphore_signal(barrier, inc=1, device_id=(partner, far_g), device_id_type=MESH)
+    pl.semaphore_wait(barrier, owners + half)
+    nearby = []
+    for at, device in enumerate([(me_a, far_g), (partner, me_g), (partner, far_g)]):
+        copy = pltpu.make_async_remote_copy(
+            src_ref=lists_ref,
+            dst_ref=near.at[at],
+            send_sem=near_send.at[at],
+            recv_sem=near_recv.at[at],
+            device_id=device,
+            device_id_type=MESH,
+        )
+        copy.start()
+        nearby.append(copy)
     copies, crossing = [], []
     for part in range(parts):
         copy = pltpu.make_async_remote_copy(
@@ -77,6 +91,27 @@
             )
         copy.start()
         copies.append(copy)
+    rows = raw_ref.shape[0]
+    index = lax.broadcasted_iota(jnp.int32, (rows, rows), 0)
+    later = jnp.where(index < lax.broadcasted_iota(jnp.int32, (rows, rows), 1), 1.0, 0.0).astype(BF)
+    owner_list = lax.broadcasted_iota(jnp.int32, (owners, rows), 0).astype(F32)
+    slot_list = lax.broadcasted_iota(jnp.int32, (half * slots, rows), 0) + base * slots
+    slot_list = slot_list.astype(F32)
+
+    def picked(owner):
+        onehot = jnp.where(owner_list == owner, 1.0, 0.0)
+        before = jnp.dot(onehot.astype(BF), later, preferred_element_type=F32)
+        slot = owner * slots + jnp.sum(before * onehot, 0, keepdims=True)
+        return jnp.where(slot_list == slot, 1.0, 0.0).astype(BF)
+
+    pick_ref[0, 0] = picked(lists_ref[2:3, :rows])
+    for copy in nearby:
+        copy.wait()
+    pick_ref[1, 0] = picked(near[0, 2:3, :rows])
+    for origin in range(2):
+        mirror = picked(near[1 + origin, 2:3, :rows])
+        mirror = jnp.dot(mirror, swap_ref[...], preferred_element_type=F32)
+        pick_ref[origin, 1] = mirror.astype(BF)
     width = 2 * KB
     for origin in range(2):
         source_g = me_g if origin == 0 else far_g
@@ -127,7 +162,7 @@
         copy.wait()
 
 
-def exchange(raw, pick, flip, lists, owners, blocks, slots):
+def exchange(raw, swap, flip, lists, owners, blocks, slots):
     rows, channels = raw.shape
     chunk = channels // CHUNKS
     vmem = pl.BlockSpec(memory_space=pltpu.VMEM)
@@ -143,6 +178,8 @@
             pltpu.VMEM((CHUNKS, rows, chunk), BF),
             pltpu.VMEM((rows, chunk), BF),
             pltpu.VMEM((CHUNKS, 2, 2, owners // 2, slots, chunk), BF),
+            pltpu.VMEM((3,) + lists.shape, F32),
+            pltpu.VMEM((2, 2, owners // 2 * slots, rows), BF),
             pltpu.SemaphoreType.DMA((CHUNKS, 2, 2, owners // 2)),
             pltpu.SemaphoreType.DMA((CHUNKS, 2, 2, owners // 2)),
             pltpu.SemaphoreType.DMA((CHUNKS, 2)),
@@ -150,12 +187,14 @@
             pltpu.SemaphoreType.DMA((CHUNKS,)),
             pltpu.SemaphoreType.DMA((owners,)),
             pltpu.SemaphoreType.DMA((owners,)),
+            pltpu.SemaphoreType.DMA((3,)),
+            pltpu.SemaphoreType.DMA((3,)),
         ],
         compiler_params=pltpu.CompilerParams(
             collective_id=0, has_side_effects=True, vmem_limit_bytes=48 * 2**20
         ),
         name="exchange",
-    )(raw, pick, flip, lists)
+    )(raw, swap, flip, lists)
 
 
 def filter_kernel(got_ref, sum_ref, high_ref, low_ref, feather_ref, out_ref, high, low):
@@ -233,37 +272,22 @@
     rows = views * rows_dev
     capacity = 2 * rows // owners
     slots = -(-capacity // 16) * 16
-    half = blocks // 2
-    other_slab = lax.ppermute(row_slab, "angle", [(s, (s + half) % blocks) for s in range(blocks)])
-    lists = jnp.concatenate([row_slab.astype(F32), row_weight.astype(F32)], 0)
-    lists = jnp.pad(lists, ((0, 0), (0, 128 - rows_dev)))
-
-    def slot_of(slab):
-        owner = slab.reshape(rows) // SLAB_DEV
-        return owner * slots + ranked(owner, owners)
-
-    pair = jnp.stack([row_slab, other_slab])
-    far = owners // 2
-    far_pair = lax.ppermute(pair, "gz", [(s, (s + far) % owners) for s in range(owners)])
-    local_partner = partner_view % views
-    is_partner = (local_partner[:, None] == jnp.arange(views)[None, :]).astype(jnp.int32)
-    slot_list = (lax.axis_index("gz") // far * far * slots + jnp.arange(far * slots))[:, None]
-
-    def picks(own_slab, partner_slab):
-        own_slot = slot_of(own_slab)
-        other_slot = slot_of(partner_slab).reshape(views, rows_dev)
-        mirror_slot = jnp.sum(is_partner[:, :, None] * other_slot[None], 1).reshape(rows)
-        return jnp.stack([own_slot[None, :] == slot_list, mirror_slot[None, :] == slot_list])
-
-    pick = jnp.stack([picks(pair[0], pair[1]), picks(far_pair[0], far_pair[1])]).astype(BF)
+    lists = jnp.stack([
+        row_slab.astype(F32).reshape(rows),
+        row_weight.astype(F32).reshape(rows),
+        (row_slab // SLAB_DEV).astype(F32).reshape(rows),
+    ])
+    lists = jnp.pad(lists, ((0, 5), (0, -rows % 128)))
+    row = jnp.arange(rows)
+    partner_row = jnp.repeat(partner_view % views, rows_dev) * rows_dev + row % rows_dev
+    swap = (row[:, None] == partner_row[None, :]).astype(BF)
     flip = (jnp.arange(KB)[:, None] + jnp.arange(KB)[None, :] == KB - 1).astype(BF)
     got, meta = exchange(
-        projections.reshape(rows, channels), pick, flip, lists, owners, blocks, slots
+        projections.reshape(rows, channels), swap, flip, lists, owners, blocks, slots
     )
-    meta = meta[:, :, :rows_dev]
-
-    all_slab = meta[:, :views].reshape(owners, rows).astype(jnp.int32)
-    all_weight = meta[:, views:].reshape(owners, rows).astype(BF)
+
+    all_slab = meta[:, 0, :rows].astype(jnp.int32)
+    all_weight = meta[:, 1, :rows].astype(BF)
     owner = all_slab // SLAB_DEV
     slot = jnp.where(owner == lax.axis_index("gz"), ranked(owner, owners), -1)
     target = jnp.arange(rows) // rows_dev * SLAB_DEV + all_slab % SLAB_DEV

time: 140 us -> 148 us (1.057)
  Pallas kernels: 125 us -> 142 us
  starting transfers between devices: 5.53 us -> 0 us
  waiting for transfers between devices: 2.04 us -> 0 us
  other arithmetic: 3.58 us -> 1.6 us
    pallas_call x1, Pallas kernels: 111 us -> 128 us  [exchange(): pl.pallas_call(functools.partial(exchange_kernel, owners, blocks, chunk),...]
    ppermute x2 -> x0, starting transfers between devices: 5.53 us -> none  [the longest x1 2.94 us: local(): lax.ppermute(row_slab, 'angle', [(s, (s + half) % blocks) for s in range(...]
    ppermute x2 -> x0, waiting for transfers between devices: 2.04 us -> none  [the longest x1 2.04 us: local(): lax.ppermute(pair, 'gz', [(s, (s + far) % owners) for s in range(owners)])]
  transfers between devices with their start and end apart: 2 -> 0, of which waited for: 1 -> 0; matrix products, arithmetic and copies ran while one was open for 2% -> 0% of each run, Pallas kernels for 0% -> 0%
where the time goes in v3:
time: 148 us
  Pallas kernels  142 us (96%)
  local copies, waits for them, and re-layouts  3.27 us (2%)
  other arithmetic  1.6 us (1%)
    pallas_call x1, Pallas kernels, exchange(): pl.pallas_call(functools.partial(exchange_kernel, owners, blocks, chunk),...  128 us
    pallas_call x1, Pallas kernels, filtered_slabs(): pl.pallas_call(filter_kernel, out_shape=jax.ShapeDtypeStruct((rows, 2 * c...  14 us

profile of v3, /device:TPU:0, one launch (start us, length us, event | category | flops | bytes accessed | tf_op | source)
XLA Modules:
  0.0 147.5 jit_solution(1192690084470279898)
XLA Ops:
  0.0 0.7 fusion.25
  0.7 0.8 reshape.83
  1.4 0.1 broadcast_in_dim.14
  1.5 0.1 mul.22
  1.6 0.8 fusion.27
  2.4 0.1 stack_reshape.12
  2.5 0.1 stack_reshape.15
  2.6 0.0 copy-start
  2.7 1.4 copy-done
  4.1 128.0 %exchange.1 = (bf16[4,2,8,48,1024]{4,3,2,1,0:T(8,128)(2,1)}, f32[8,8,256]{2,1,0:T(8,128)S(1)}) custom-call(bf16[192,4096]{1,0:T(8,128)(2,1)S(1)} %bitcast.39, bf16[192,192]{1,0:T(8,128)(2,1)S(1)} %fusion.9.swap_ref, bf16[256,256]{1,0:T(8,128)(2,1)S(1)} %fusion.7.flip_ref, f32[8,256]{1,0:T(8,128)S(1)} %select_maximum_fusion.lists_ref), custom_call_target="tpu_custom_call" | custom-call | tf_op jit(solution)/shard_map/exchange/pallas_call | solution.py:169
  132.2 0.2 fusion.2
  132.4 0.4 convolution_convert_fusion
  132.7 0.8 copy.10.sum_ref
  133.5 14.0 %filter.1 = bf16[192,8192]{1,0:T(8,128)(2,1)} custom-call(bf16[4,2,384,1024]{3,2,1,0:T(8,128)(2,1)} %bitcast.40, bf16[192,384]{1,0:T(8,128)(2,1)} %copy.10.sum_ref, bf16[768,256]{1,0:T(8,128)(2,1)} %constant.89.clone.high_ref, bf16[768,256]{1,0:T(8,128)(2,1)} %constant.90.clone.low_ref, f32[1,256]{1,0:T(1,128)} %constant.88.clone.feather_ref), custom_call_target="tpu_custom_call" | custom-call | tf_op jit(solution)/shard_map/filter/pallas_call | solution.py:250
  (12 shorter events, 0.2 us)
Async XLA Ops:
  2.6 1.4 copy-start

commit v4 on v2

--- a/solution.py
+++ b/solution.py
@@ -244,7 +244,14 @@
 
     pair = jnp.stack([row_slab, other_slab])
     far = owners // 2
-    far_pair = lax.ppermute(pair, "gz", [(s, (s + far) % owners) for s in range(owners)])
+    shift = [(s, (s + far) % owners) for s in range(owners)]
+    both = [
+        (s * owners + t, (s + half) % blocks * owners + (t + far) % owners)
+        for s in range(blocks) for t in range(owners)
+    ]
+    far_pair = [
+        lax.ppermute(row_slab, "gz", shift), lax.ppermute(row_slab, ("angle", "gz"), both)
+    ]
     local_partner = partner_view % views
     is_partner = (local_partner[:, None] == jnp.arange(views)[None, :]).astype(jnp.int32)
     slot_list = (lax.axis_index("gz") // far * far * slots + jnp.arange(far * slots))[:, None]

time: 140 us -> 138 us (0.986)
    ppermute x1 -> x2, starting transfers between devices: 2.59 us -> 4.07 us  [the longest x1 4.04 us: local(): lax.ppermute(row_slab, 'gz', shift)]
    ppermute x1, starting transfers between devices: 2.94 us -> 1.49 us  [local(): lax.ppermute(row_slab, 'angle', [(s, (s + half) % blocks) for s in range(...]
  transfers between devices with their start and end apart: 2 -> 3, of which waited for: 1 -> 1; matrix products, arithmetic and copies ran while one was open for 2% -> 3% of each run, Pallas kernels for 0% -> 0%
where the time goes in v4:
time: 138 us; the launch traced here: 137 us
  Pallas kernels  124 us (90%)
  starting transfers between devices  5.56 us (4%)
  other arithmetic  2.86 us (2%)
  local copies, waits for them, and re-layouts  2.33 us (2%)
  waiting for transfers between devices  1.74 us (1%)
    pallas_call x1, Pallas kernels, exchange(): pl.pallas_call(functools.partial(exchange_kernel, owners, blocks, chunk),...  110 us
    pallas_call x1, Pallas kernels, filtered_slabs(): pl.pallas_call(filter_kernel, out_shape=jax.ShapeDtypeStruct((rows, 2 * c...  14 us
    ppermute x1, starting transfers between devices, local(): lax.ppermute(row_slab, 'gz', shift)  4.04 us
  transfers between devices with their start and end apart: 3, of which 1 were waited for; matrix products, arithmetic and copies ran while one was open for 3% of the time, Pallas kernels for 0%

profile of v4, /device:TPU:0, one launch (start us, length us, event | category | flops | bytes accessed | tf_op | source)
XLA Modules:
  0.0 137.5 jit_solution(13401405439504697997)
XLA Ops:
  0.0 0.0 copy-start
  0.0 4.0 %collective-permute-start.1 = (s32[12,16]{1,0:T(8,128)}, s32[12,16]{1,0:T(8,128)S(1)}, u32[]{:S(2)}, u32[]{:S(2)}) collective-permute-start(s32[12,16]{1,0:T(8,128)} %param.10), channel_id=1, source_target_pairs={{0,4},{1,5},{2,6},{3,7},{4,0},{5,1},{6,2},{7,3},{8,12},{9,13},{10,... | collective-permute-start | bytes 2312 | tf_op jit(solution)/shard_map/ppermute | solution.py:253
  4.0 1.5 %collective-permute-start = (s32[12,16]{1,0:T(8,128)}, s32[12,16]{1,0:T(8,128)S(1)}, u32[]{:S(2)}, u32[]{:S(2)}) collective-permute-start(s32[12,16]{1,0:T(8,128)} %param.10), channel_id=1, source_target_pairs={{0,16},{8,24},{16,0},{24,8},{1,17},{9,25},{17,1},{25,9},{2,18},{10... | collective-permute-start | bytes 2312 | tf_op jit(solution)/shard_map/ppermute | solution.py:237
  5.5 0.0 collective-permute-start.2
  5.6 0.8 reshape_squeeze_stack.6
  6.4 0.7 convert_element_type.144
  7.1 0.7 and_select_fusion.4
  7.8 0.2 fusion.3
  8.0 0.1 fusion.28
  8.1 0.7 convert_element_type.145
  8.8 0.0 collective-permute-done.1
  8.8 0.1 reshape.528
  8.9 0.2 fusion.5
  9.1 0.0 collective-permute-done
  9.1 0.1 reshape_squeeze_stack.7
  9.2 0.2 fusion.4
  9.4 0.1 convert_element_type.134
  9.5 1.7 %collective-permute-done.2 = s32[12,16]{1,0:T(8,128)S(1)} collective-permute-done((s32[12,16]{1,0:T(8,128)}, s32[12,16]{1,0:T(8,128)S(1)}, u32[]{:S(2)}, u32[]{:S(2)}) %collective-permute-start.2) | collective-permute-done | bytes 800 | tf_op jit(solution)/shard_map/ppermute | solution.py:253
  11.2 0.1 reshape.529
  11.3 0.2 fusion.6
  11.5 0.1 convert_element_type.141
  11.6 0.1 multiply_reduce_fusion.1
  11.7 0.1 eq.218
  11.8 0.1 eq.229
  11.9 0.2 broadcast_compare_fusion.3
  12.1 0.1 add_bitcast_fusion
  12.2 0.1 add_convert_fusion.pick_ref
  12.3 0.0 copy-done
  12.3 109.6 %exchange.1 = (bf16[4,2,8,48,1024]{4,3,2,1,0:T(8,128)(2,1)}, f32[8,24,128]{2,1,0:T(8,128)S(1)}) custom-call(bf16[192,4096]{1,0:T(8,128)(2,1)S(1)} %bitcast.19, bf16[2,2,192,192]{3,2,1,0:T(8,128)(2,1)S(1)} %add_convert_fusion.pick_ref, bf16[256,256]{1,0:T(8,128)(2,1)S(1)} %fusion.11.flip_ref, f32[24,128]{1,0:T(8,128)S(1)} %select_maximum_fusion.lists_ref), custom_call_target="tpu_custom_call" | custom-call | tf_op jit(solution)/shard_map/exchange/pallas_call | solution.py:134
  121.9 0.1 convert_element_type.147
  122.0 0.1 convert_element_type.151
  122.1 0.2 fusion.2
  122.3 0.4 convolution_convert_fusion
  122.7 0.8 copy.10.sum_ref
  123.5 14.0 %filter.1 = bf16[192,8192]{1,0:T(8,128)(2,1)} custom-call(bf16[4,2,384,1024]{3,2,1,0:T(8,128)(2,1)} %bitcast.20, bf16[192,384]{1,0:T(8,128)(2,1)} %copy.10.sum_ref, bf16[768,256]{1,0:T(8,128)(2,1)} %constant.117.clone.high_ref, bf16[768,256]{1,0:T(8,128)(2,1)} %constant.118.clone.low_ref, f32[1,256]{1,0:T(1,128)} %constant.116.clone.feather_ref), custom_call_target="tpu_custom_call" | custom-call | tf_op jit(solution)/shard_map/filter/pallas_call | solution.py:211
  (18 shorter events, 0.3 us)
Async XLA Ops:
  0.0 12.3 %copy-start = (bf16[12,16,4096]{2,1,0:T(8,128)(2,1)S(1)}, bf16[12,16,4096]{2,1,0:T(8,128)(2,1)}, u32[]{:S(2)}) copy-start(bf16[12,16,4096]{2,1,0:T(8,128)(2,1)} %param.7) | copy-start | bytes 4718596
  0.0 8.8 %collective-permute-start.1 = (s32[12,16]{1,0:T(8,128)}, s32[12,16]{1,0:T(8,128)S(1)}, u32[]{:S(2)}, u32[]{:S(2)}) collective-permute-start(s32[12,16]{1,0:T(8,128)} %param.10), channel_id=1, source_target_pairs={{0,4},{1,5},{2,6},{3,7},{4,0},{5,1},{6,2},{7,3},{8,12},{9,13},{10,... | collective-permute-start | bytes 2312 | tf_op jit(solution)/shard_map/ppermute | solution.py:253
  4.0 5.1 %collective-permute-start = (s32[12,16]{1,0:T(8,128)}, s32[12,16]{1,0:T(8,128)S(1)}, u32[]{:S(2)}, u32[]{:S(2)}) collective-permute-start(s32[12,16]{1,0:T(8,128)} %param.10), channel_id=1, source_target_pairs={{0,16},{8,24},{16,0},{24,8},{1,17},{9,25},{17,1},{25,9},{2,18},{10... | collective-permute-start | bytes 2312 | tf_op jit(solution)/shard_map/ppermute | solution.py:237
  5.5 5.7 %collective-permute-start.2 = (s32[12,16]{1,0:T(8,128)}, s32[12,16]{1,0:T(8,128)S(1)}, u32[]{:S(2)}, u32[]{:S(2)}) collective-permute-start(s32[12,16]{1,0:T(8,128)} %param.10), channel_id=1, source_target_pairs={{0,20},{1,21},{2,22},{3,23},{4,16},{5,17},{6,18},{7,19},{8,28},{9,... | collective-permute-start | bytes 2312 | tf_op jit(solution)/shard_map/ppermute | solution.py:253
